TPU v7x, 128 devices: a whole 4x4x4 slice. The times are simulated.
128 devices in a mesh: dp: 2 (over core), row: 8 (over x_lo, y), col: 8 (over z, x_hi).
Axes of the slice: x: 4 (x_hi: 2, x_lo: 2; x = x_hi * 2 + x_lo), y: 4, z: 4, core: 2. Of those that a mesh axis runs over, the one named last changes fastest.
Arguments:
- expected: bfloat16 [4096, 8192], P(('dp', 'col'), 'row'), may hold values from -6 to 6
- labels: int32 [4096], replicated, may hold values from 0 to 65535
- unembedding: bfloat16 [65536, 8192], P(('dp', 'col'), 'row'), may hold values from -6 to 6
- down_weight: bfloat16 [28672, 8192], P('col', 'row'), may hold values from -0.0625 to 0.0625
Outputs:
- hidden_grad: bfloat16 [4096, 28672], P(('dp', 'row'), 'col')
- fisher_factor: float32 [8192, 8192], P('row', ('dp', 'col'))
All inputs are finite; a program needn't handle non-finite values.
Results may differ from a plain program's by a relative error of at most 0.0051.
Values may be sent and summed in bfloat16 or wider, within the bound.
A program may use at most 256 MiB of HBM per device.

v0:
```python
import jax
import jax.numpy as jnp
from jax import lax
from jax.sharding import PartitionSpec as P


def shards(expected, labels, unembedding, down_weight):
    col_size = lax.axis_size("col")
    tile_tokens = expected.shape[0]
    voc_shard = unembedding.shape[0]
    replica = lax.axis_index("dp")
    col_place = lax.axis_index("col")
    group_place = replica * col_size + col_place
    replica_tokens = tile_tokens * col_size
    local_ids = labels - group_place * voc_shard
    inside_shard = (local_ids >= 0) & (local_ids < voc_shard)
    picked = jnp.take(unembedding, jnp.clip(local_ids, 0, voc_shard - 1), axis=0)
    label_sum = lax.psum(
        jnp.where(inside_shard[:, None], picked.astype(jnp.float32), 0.0).astype(jnp.bfloat16),
        ("dp", "col"),
    ).astype(jnp.float32)
    gathered = lax.all_gather(expected, ("dp", "col"), axis=0, tiled=True)
    grad_all = (gathered.astype(jnp.float32) - label_sum).astype(jnp.bfloat16)
    grad_tile = lax.dynamic_slice_in_dim(grad_all, group_place * tile_tokens, tile_tokens, 0)
    replica_panel = lax.dynamic_slice_in_dim(grad_all, replica * replica_tokens, replica_tokens, 0)
    contract_last = (((1,), (1,)), ((), ()))
    hidden_sum = lax.psum_scatter(
        lax.dot_general(
            replica_panel, down_weight, contract_last, preferred_element_type=jnp.float32
        ),
        "row",
        scatter_dimension=0,
        tiled=True,
    )
    hidden_grad = hidden_sum.astype(jnp.bfloat16)
    wide_tile = lax.all_gather(grad_tile, "row", axis=1, tiled=True)
    owned_columns = lax.all_to_all(
        wide_tile, ("dp", "col"), split_axis=1, concat_axis=0, tiled=True
    )
    total_tokens = grad_all.shape[0]
    fisher_factor = (
        lax.dot_general(
            grad_all, owned_columns, (((0,), (0,)), ((), ())), preferred_element_type=jnp.float32
        )
        / total_tokens
    )
    return (hidden_grad, fisher_factor)


def solution(mesh):
    in_specs = (P(("dp", "col"), "row"), P(), P(("dp", "col"), "row"), P("col", "row"))
    out_specs = (P(("dp", "row"), "col"), P("row", ("dp", "col")))
    return jax.shard_map(shards, mesh=mesh, in_specs=in_specs, out_specs=out_specs, check_vma=False)
```

profile of v0, /device:TPU:38, one launch (start us, length us, event | category | flops | bytes accessed | tf_op | source)
XLA Modules:
  0.0 890.4 jit_solution(2499190441615694398)
XLA Ops:
  7.2 0.0 all-reduce.2.cloned.1.call-start
  7.2 0.7 compare_and_fusion.1
  8.0 0.7 fusion.2
  8.7 25.3 %gather_fusion = bf16[4096,1024]{1,0:T(8,128)(2,1)} fusion(bf16[4096,1024]{1,0:T(8,128)(2,1)} %param.6, s32[4096]{0:T(1024)S(1)} %fusion.2), kind=kCustom, calls=%fused_computation | custom fusion | bytes 16793600 | tf_op jit(solution)/shard_map/jit(_take)/gather | solution.py:17
  34.0 7.8 select_convert_fusion
  41.9 0.0 all-reduce.2.cloned.1.call-update
  41.9 0.0 all-gather.3.cloned.1.call-start
  42.0 0.7 all-gather.3.cloned.1.call-update
  42.7 0.0 all-gather.5.cloned.1.call-start
  42.7 364.7 %all-reduce.2.cloned.1.call-done = bf16[4096,1024]{1,0:T(8,128)(2,1)} async-done(((bf16[4096,1024]{1,0:T(8,128)(2,1)}), bf16[4096,1024]{1,0:T(8,128)(2,1)}) %all-reduce.2.cloned.1.call-update) | async-done | bytes 8388624 | tf_op jit(solution)/shard_map/psum | solution.py:18
  407.4 73.3 %all-gather.3.cloned.1.call-done = bf16[4096,1024]{1,0:T(8,128)(2,1)} async-done(((bf16[256,1024]{1,0:T(8,128)(2,1)}), bf16[4096,1024]{1,0:T(8,128)(2,1)}) %all-gather.3.cloned.1.call-update) | async-done | bytes 8388624 | tf_op jit(solution)/shard_map/all_gather | solution.py:22
  480.8 7.9 subtract_convert_fusion
  488.7 0.0 copy-start
  488.7 3.3 copy-done
  492.0 0.8 constant_dynamic-slice_fusion
  492.8 0.0 all-gather.5.cloned.1.call-update
  492.9 0.0 reduce-scatter.2.cloned.1.call-start
  492.9 23.1 %fusion = f32[2048,3584]{1,0:T(8,128)} fusion(bf16[3584,1024]{1,0:T(8,128)(2,1)} %param.7, bf16[4096,1024]{1,0:T(8,128)(2,1)} %copy-done, s32[]{:T(128)S(6)} %select_n.22), kind=kOutput, calls=%fused_computation.4 | convolution fusion | flops 15032385536 | bytes 40894468 | tf_op jit(solution)/shard_map/dot_general | solution.py:28
  516.0 0.0 reduce-scatter.2.cloned.1.call-update
  516.0 29.6 %all-gather.5.cloned.1.call-done = bf16[256,8192]{1,0:T(8,128)(2,1)} async-done(((bf16[256,1024]{1,0:T(8,128)(2,1)}), bf16[256,8192]{1,0:T(8,128)(2,1)}) %all-gather.5.cloned.1.call-update) | async-done | bytes 4194320 | tf_op jit(solution)/shard_map/all_gather | solution.py:36
  545.7 0.0 slice-start
  545.7 2.8 copy.9
  548.5 0.0 slice-start.1
  548.5 99.9 %all_to_all.19 = bf16[256,16,512]{2,0,1:T(8,128)(2,1)S(1)} all-to-all(bf16[256,16,512]{2,0,1:T(8,128)(2,1)S(1)} %bitcast.10), channel_id=1, replica_groups=mesh['dp'=2,'row'=8,'col'=8] {'dp','col'}, dimensions={1} | all-to-all | bytes 8388608 | tf_op jit(solution)/shard_map/all_to_all | solution.py:37
  648.4 0.0 slice-done
  648.4 0.0 slice-done.1
  648.4 5.8 convolution_multiply_fusion
  654.2 226.1 %reduce-scatter.2.cloned.1.call-done = f32[256,3584]{1,0:T(8,128)} async-done(((f32[2048,3584]{1,0:T(8,128)}), f32[256,3584]{1,0:T(8,128)}) %reduce-scatter.2.cloned.1.call-update) | async-done | bytes 3670032 | tf_op jit(solution)/shard_map/reduce_scatter | solution.py:27
  880.4 3.4 convert_element_type.23
  (1 shorter events, 0.0 us)
Async XLA Ops:
  7.2 400.3 %all-reduce.2.cloned.1.call-start = ((), (), s32[]{:S(2)}) async-start(), calls=%async_computation.3 | async-start | bytes 16777216 | tf_op jit(solution)/shard_map/psum | solution.py:18
  41.9 438.9 %all-gather.3.cloned.1.call-start = ((), (), s32[]{:S(2)}) async-start(), calls=%async_computation.2 | async-start | bytes 8912896 | tf_op jit(solution)/shard_map/all_gather | solution.py:22
  42.7 503.0 %all-gather.5.cloned.1.call-start = ((), (), s32[]{:S(2)}) async-start(), calls=%async_computation.5 | async-start | bytes 4718592 | tf_op jit(solution)/shard_map/all_gather | solution.py:36
  488.7 3.4 copy-start
  492.9 387.5 %reduce-scatter.2.cloned.1.call-start = ((), (), s32[]{:S(2)}) async-start(), calls=%async_computation.4 | async-start | bytes 33030144 | tf_op jit(solution)/shard_map/reduce_scatter | solution.py:27
  545.7 102.7 %slice-start = ((s8[8388608]{0:T(1024)(128)(4,1)}), s8[4194304]{0:T(1024)(128)(4,1)S(1)}, s32[]{:S(2)}) async-start(s8[8388608]{0:T(1024)(128)(4,1)} %bitcast.11), calls=%async_computation.6 | async-start | bytes 8388608
  548.5 99.9 %slice-start.1 = ((s8[8388608]{0:T(1024)(128)(4,1)}), s8[4194304]{0:T(1024)(128)(4,1)S(1)}, s32[]{:S(2)}) async-start(s8[8388608]{0:T(1024)(128)(4,1)} %bitcast.11), calls=%async_computation.7 | async-start | bytes 8388608
Sparse Core Ops, SparseCore 0:
  42.0 365.3 all-reduce.1
  409.9 70.8 all-gather.2
  493.0 52.6 all-gather.4
  548.0 332.3 reduce-scatter.1
where the time goes:
time: 892 us; the launch traced here: 890 us
  waiting for transfers between devices  695 us (78%)
  blocking collectives  99.9 us (11%)
  local copies, waits for them, and re-layouts  32.3 us (4%)
  matrix products  28.9 us (3%)
  other arithmetic  20.6 us (2%)
  between operations  13.8 us (2%)
    psum x1, waiting for transfers between devices, shards(): lax.psum(jnp.where(inside_shard[:, None], picked.astype(jnp.float32), 0.0...  365 us
    reduce_scatter x1, waiting for transfers between devices, shards(): lax.psum_scatter(lax.dot_general(replica_panel, down_weight, contract_las...  226 us
    all_to_all x1, blocking collectives, shards(): lax.all_to_all(wide_tile, ('dp', 'col'), split_axis=1, concat_axis=0, til...  99.9 us
    all_gather x1, waiting for transfers between devices, shards(): gathered = lax.all_gather(expected, ('dp', 'col'), axis=0, tiled=True)  73.3 us
    all_gather x1, waiting for transfers between devices, shards(): wide_tile = lax.all_gather(grad_tile, 'row', axis=1, tiled=True)  29.6 us
    gather x1, local copies, waits for them, and re-layouts, shards(): jnp.take(unembedding, jnp.clip(local_ids, 0, voc_shard - 1), axis=0)  25.3 us
    dot_general x1, matrix products, shards(): lax.dot_general(replica_panel, down_weight, contract_last, preferred_elem...  23.1 us
  transfers between devices with their start and end apart: 4, of which 4 were waited for; matrix products, arithmetic and copies ran while one was open for 4% of the time, Pallas kernels for 0%

commit v1 on v0

v1 whole, which is shorter than its diff:
```python
import jax
import jax.numpy as jnp
from jax import lax
from jax.experimental import pallas as pl
from jax.experimental.pallas import tpu as pltpu
from jax.sharding import PartitionSpec as P

CAP = 32
EARLY = 3
F_AT = 5
TILE = 256
DEPTH = 512
PART = 128
UNITS = 2 * (TILE // PART)
MESH = pl.DeviceIdType.MESH


def dense_rows(ids, unembedding, place):
    ring = lax.axis_size("dp") * lax.axis_size("col")
    voc_shard = unembedding.shape[0]
    tokens = ids.shape[1]

    def held(k):
        block = lax.rem(place + 2 * ring - 1 - k, ring)
        local = lax.dynamic_slice_in_dim(ids, block, 1, 0).reshape(tokens) - place * voc_shard
        inside = (local >= 0) & (local < voc_shard)
        rows = jnp.take(unembedding, jnp.clip(local, 0, voc_shard - 1), axis=0, mode="clip")
        return jnp.where(inside[:, None], rows, jnp.zeros_like(rows))

    def step(k, total):
        moved = lax.ppermute(total, ("dp", "col"), [(i, (i + 1) % ring) for i in range(ring)])
        return moved + held(k)

    return lax.fori_loop(1, ring, step, held(0))


def dot_nt(x, w):
    return lax.dot_general(x, w, (((1,), (1,)), ((), ())), preferred_element_type=jnp.float32)


def dot_tn(x, w):
    return lax.dot_general(x, w, (((0,), (0,)), ((), ())), preferred_element_type=jnp.float32)


def kernel(
    row_ref, slot_ref, exp_ref, extra_ref, u_ref, w_ref,
    hid_ref, fis_out, f_in,
    u_rest, lab_out, lab_in, grad_own, g_all, g_sib, g_col, c_mid, w_own, w_part,
    tr_out, tr_in, pl_out, pl_in, cb_out, cb_in, own_sum, fis_ref, f_out,
    u_s, lab_ss, lab_rs, wl_s, wd_ss, wd_rs, wf_ss, wf_rs, gx_ss, g_rs, gz_ss,
    tr_ss, tr_rs, pl_ss, pl_rs, cb_ss, cb_rs, sib_ss, sib_rs, cy_ss, cy_rs, col_ss, col_rs, f_ss, f_rs, fis_s,
):
    d = lax.axis_index("dp")
    r = lax.axis_index("row")
    c = lax.axis_index("col")
    a, y = r // 4, r % 4
    z, b = c // 2, c % 2
    v = d * 8 + c
    half = w_ref.shape[0] // 2
    n_chunk = half // TILE
    a_to = z // 2

    def dev(d_, a_, y_, z_, b_):
        return {"dp": d_, "row": a_ * 4 + y_, "col": z_ * 2 + b_}

    def rc(src, dst, ss, rs, to):
        return pltpu.make_async_remote_copy(
            src_ref=src, dst_ref=dst, send_sem=ss, recv_sem=rs, device_id=to, device_id_type=MESH
        )

    def loop(n, body, start=0):
        def step(i, carry):
            body(i)
            return carry

        lax.fori_loop(start, n, step, 0)

    sibling = dev(1 - d, a, y, z, b)
    partner = dev(d, 1 - a, y, z, b)

    bar = pltpu.get_barrier_semaphore()

    def hello(to):
        pl.semaphore_signal(bar, inc=1, device_id=to, device_id_type=MESH)

    def group_dev(k):
        w = lax.rem(v + k, 16)
        return {"dp": w // 8, "row": r, "col": lax.rem(w, 8)}

    loop(16, lambda k: hello(group_dev(k)), 1)
    loop(8, lambda k: hello({"dp": d, "row": (1 - a) * 4 + y, "col": k}))
    up_y = dev(d, a, lax.rem(y + 1, 4), z, b)
    dn_y = dev(d, a, lax.rem(y + 3, 4), z, b)
    hello(up_y)
    hello(dn_y)
    hello(dev(d, a, lax.rem(y + 2, 4), z, b))

    def w_rows(i, h):
        return pl.ds(pl.multiple_of((d if h == 0 else 1 - d) * half + i * TILE, TILE), TILE)

    def wd_copy(i):
        rows = w_rows(i, 0)
        return rc(w_ref.at[rows], w_part.at[rows], wd_ss.at[i], wd_rs.at[i], partner)

    def wf_copy(i):
        rows = w_rows(i, 0)
        return rc(w_part.at[rows], w_part.at[rows], wf_ss.at[i], wf_rs.at[i], sibling)

    def wf_wait(i):
        rows = w_rows(i, 1)
        rc(w_part.at[rows], w_part.at[rows], wf_ss.at[i], wf_rs.at[i], sibling).wait_recv()

    depth = u_rest.shape[0]
    n_deep = u_ref.shape[0] // depth

    def u_load(k):
        src = u_ref.at[pl.ds(pl.multiple_of(k * depth, depth), depth)]
        return pltpu.make_async_copy(src, w_own.at[pl.ds(pl.multiple_of(k * depth, depth), depth)], u_s.at[k])

    u_last = pltpu.make_async_copy(u_ref.at[pl.ds((n_deep - 1) * depth, depth)], u_rest, u_s.at[n_deep - 1])
    loop(n_deep - 1, lambda k: u_load(k).start())
    u_last.start()

    def choose(k, held, fresh):
        rows = held[...]
        for m in range(lab_out.shape[0] // TILE):
            wanted = row_ref[:, m * TILE:(m + 1) * TILE] - k * depth
            pick = jnp.where(
                lax.broadcasted_iota(jnp.int32, (depth, TILE), 0) == wanted, 1.0, 0.0
            ).astype(jnp.bfloat16)
            for n in range(rows.shape[1] // TILE):
                found = dot_tn(pick, rows[:, n * TILE:(n + 1) * TILE])
                own_sum[m, n] = found if fresh else own_sum[m, n] + found

    u_last.wait()
    choose(n_deep - 1, u_rest, True)
    pl.semaphore_wait(bar, 26)

    def choose_next(k):
        u_load(k).wait()
        choose(k, w_own.at[pl.ds(pl.multiple_of(k * depth, depth), depth)], False)

    loop(n_deep - 1, choose_next)
    for m in range(lab_out.shape[0] // TILE):
        for n in range(lab_out.shape[1] // TILE):
            lab_out[m * TILE:(m + 1) * TILE, n * TILE:(n + 1) * TILE] = own_sum[m, n].astype(jnp.bfloat16)
    w_load = pltpu.make_async_copy(w_ref, w_own, wl_s)
    w_load.start()

    width = lab_in.shape[1] // 2

    def side(f):
        return pl.ds(pl.multiple_of(f * width, width), width)

    def lab_copy(k, f):
        w = lax.rem(v + k, 16)
        return rc(
            lab_out.at[pl.ds(pl.multiple_of(w * CAP, CAP), CAP), side(f)],
            lab_in.at[pl.ds(pl.multiple_of(v * CAP, CAP), CAP), side(f)],
            lab_ss.at[f, k], lab_rs.at[f, k], group_dev(k),
        )

    mine = pl.ds(pl.multiple_of(v * CAP, CAP), CAP)
    lab_local = pltpu.make_async_copy(lab_out.at[mine], lab_in.at[mine], lab_rs.at[0, 0])
    lab_local.start()
    for f in range(2):
        loop(16, lambda k: lab_copy(k, f).start(), 1)

    def lab_wait(k, f):
        w = lax.rem(v + 16 - k, 16)
        rows = pl.ds(pl.multiple_of(w * CAP, CAP), CAP)
        rc(
            lab_in.at[rows, side(f)], lab_in.at[rows, side(f)], lab_ss.at[f, k], lab_rs.at[f, k],
            {"dp": w // 8, "row": r, "col": lax.rem(w, 8)},
        ).wait_recv()

    lab_local.wait()
    n_slot = lab_in.shape[0]
    chosen = jnp.where(
        lax.broadcasted_iota(jnp.int32, (n_slot, TILE), 0) == slot_ref[...], 1.0, 0.0
    ).astype(jnp.bfloat16)

    def make_grad(n):
        cols = pl.ds(pl.multiple_of(n * TILE, TILE), TILE)
        rows = dot_tn(chosen, lab_in[:, cols])
        rows = rows + extra_ref[:, cols].astype(jnp.float32)
        grad_own[:, cols] = (exp_ref[:, cols].astype(jnp.float32) - rows).astype(jnp.bfloat16)

    def grad_side(f):
        loop(16, lambda k: lab_wait(k, f), 1)
        loop((f + 1) * (width // TILE), make_grad, f * (width // TILE))

    n_part = TILE // PART
    kk = jnp.where(a == a_to, 0, 1)

    def part_rows(block, s):
        return pl.ds(pl.multiple_of(block * TILE + s * PART, PART), PART)

    def gx_parts(f, s):
        src = grad_own.at[part_rows(0, s), side(f)]
        dst = g_all.at[kk, part_rows(lax.rem(z, 2) * 2 + b, s), side(f)]
        sem = g_rs.at[lax.rem(z, 2) * 4 + b * 2 + kk, f * n_part + s]
        near = rc(src, dst, gx_ss.at[0, f * n_part + s], sem, partner)
        far = rc(src, dst, gx_ss.at[1, f * n_part + s], sem, dev(d, a_to, y, z, 1 - b))
        return near, far, (src, dst, sem)

    def gx_start(f, s):
        near, far, here = gx_parts(f, s)

        @pl.when(a == a_to)
        def _():
            pltpu.make_async_copy(*here).start()

        @pl.when(a != a_to)
        def _():
            near.start()

        far.start()

    zeta = lax.rem(z - 2 * a + 4, 4)
    first = lax.rem((zeta + 1) // 2, 2)
    up_z = dev(d, a, y, lax.rem(z + 1, 4), b)
    dn_z = dev(d, a, y, lax.rem(z + 3, 4), b)

    def g_copy(par, q, f, s, way):
        block = g_all.at[lax.rem(q, 2), part_rows(par * 2 + q // 2, s), side(f)]
        u = f * n_part + s
        return rc(
            block, block, gz_ss.at[way, q, u], g_rs.at[par * 4 + q, u], up_z if way == 0 else dn_z
        )

    def g_order(i):
        return jnp.where(i < 2, b, 1 - b) * 2 + ((i + 1) // 2) % 2

    def unit(t):
        u = lax.rem(t, 2 * UNITS)
        return g_order(t // (2 * UNITS) * 2 + lax.rem(u // n_part, 2)), u // UNITS, lax.rem(u, n_part)

    def relay(t):
        q, f, s = unit(t)
        g_copy(first, q, f, s, 0).wait_recv()

        @pl.when(zeta != 3)
        def _():
            g_copy(first, q, f, s, 0).start()

        @pl.when(zeta != 2)
        def _():
            g_copy(first, q, f, s, 1).start()

    grad_side(0)
    loop(n_part, lambda s: gx_start(0, s))

    @pl.when(zeta < 2)
    def _():
        loop(n_part, relay)

    grad_side(1)
    loop(n_part, lambda s: gx_start(1, s))
    loop(n_chunk, lambda i: wd_copy(i).start())

    def partial(y_, i, h):
        rows = pl.ds(pl.multiple_of(y_ * TILE, TILE), TILE)
        wr = w_rows(i, h)
        return dot_nt(g_all[0, rows, :], w_own[wr, :]) + dot_nt(g_all[1, rows, :], w_part[wr, :])

    def ahead(h):
        return up_y if h == 0 else dn_y

    def behind(h):
        return dn_y if h == 0 else up_y

    def y_off(h, n):
        return lax.rem(y + (n if h == 0 else 4 - n), 4)

    def tr_copy(i, h):
        return rc(tr_out.at[h, i], tr_in.at[h, i], tr_ss.at[h, i], tr_rs.at[h, i], ahead(h))

    def pl_copy(i, h):
        return rc(pl_out.at[h, i], pl_in.at[h, i], pl_ss.at[h, i], pl_rs.at[h, i], behind(h))

    def cb_copy(i, h):
        return rc(cb_out.at[h, i], cb_in.at[h, i], cb_ss.at[h, i], cb_rs.at[h, i], ahead(h))

    def transit(i, h):
        tr_out[h, i] = partial(y_off(h, 2), i, h).astype(jnp.bfloat16)
        tr_copy(i, h).start()

    def plain(i, h):
        pl_out[h, i] = partial(y_off(h, 3), i, h).astype(jnp.bfloat16)
        pl_copy(i, h).start()

    def keep(i, h):
        own_sum[h, i] = partial(y, i, h)

    def combine(i, h):
        part = partial(y_off(h, 1), i, h)
        tr_copy(i, h).wait_recv()
        cb_out[h, i] = (part + tr_in[h, i].astype(jnp.float32)).astype(jnp.bfloat16)
        cb_copy(i, h).start()


    def col_row(zeta_):
        near = lax.rem((zeta_ + 1) // 2, 2)
        side = jnp.where(zeta_ < 2, 1 - b, b)
        return pl.ds(pl.multiple_of((near * 2 + side) * TILE, TILE), TILE)

    z_row = col_row(zeta)
    b_cols = side(b)

    def cy_copy(n, d_):
        src = g_all.at[jnp.where(d_ == a, 0, 1), z_row, b_cols]
        return rc(src, c_mid.at[n - 1, d_], cy_ss.at[n - 1, d_], cy_rs.at[n - 1, d_],
                  dev(d, a, lax.rem(y + n, 4), z, b))

    def cy_each(act):
        def step(k):
            act(cy_copy(k // 2 + 1, lax.rem(k, 2)))

        loop(6, step)

    @pl.when(zeta >= 2)
    def _():
        loop(2 * UNITS, relay)
        cy_each(lambda copy: copy.start())

    @pl.when(zeta < 2)
    def _():
        loop(4 * UNITS, relay, n_part)
        cy_each(lambda copy: copy.start())

    def second_wait(t):
        g_copy(1 - first, *unit(t), 0).wait_recv()

    loop(2 * UNITS, second_wait)
    w_load.wait()
    even = lax.rem(y, 2) == b

    def early_step(i):
        wd_copy(i).wait_recv()
        wf_copy(i).start()
        for h in range(2):
            if h == 1:
                wf_wait(i)

            @pl.when(even)
            def _():
                transit(i, h)
                keep(i, h)

            @pl.when(jnp.logical_not(even))
            def _():
                plain(i, h)

                @pl.when(i > 0)
                def _():
                    combine(i - 1, h)

        @pl.when(jnp.logical_and(zeta >= 2, i < 2))
        def _():
            loop((3 + i) * UNITS, relay, (2 + i) * UNITS)

    loop(EARLY, early_step)
    loop(4 * UNITS, second_wait, 2 * UNITS)
    sib_copy = rc(g_all, g_sib, sib_ss, sib_rs, sibling)
    sib_copy.start()

    def cz_parts(k):
        n, d_ = k // 2, lax.rem(k, 2)
        z_to = lax.rem(y + 4 - n, 4)
        dst = g_col.at[d, z_row]
        sem = col_rs.at[d * 4 + zeta]
        mid = c_mid.at[jnp.maximum(n - 1, 0), d_]
        own = g_all.at[jnp.where(d_ == a, 0, 1), z_row, b_cols]
        is_self = jnp.logical_and(z_to == z, d_ == d)
        to = dev(d_, a, y, z_to, b)
        return n, is_self, mid, own, dst, sem, to

    def cz_start(k):
        n, is_self, mid, own, dst, sem, to = cz_parts(k)
        for src, has in ((own, n == 0), (mid, n > 0)):
            @pl.when(jnp.logical_and(has, is_self))
            def _():
                pltpu.make_async_copy(src, dst, sem).start()

            @pl.when(jnp.logical_and(has, jnp.logical_not(is_self)))
            def _():
                rc(src, dst, col_ss.at[k], sem, to).start()

    cy_each(lambda copy: copy.wait_recv())
    loop(8, cz_start)

    lag = 1

    @pl.when(jnp.logical_not(even))
    def _():
        for h in range(2):
            combine(EARLY - 1, h)

    def other_step(i):
        for h in range(2):

            @pl.when(even)
            def _():
                plain(i, h)

            @pl.when(jnp.logical_not(even))
            def _():
                transit(i, h)
                keep(i, h)

    loop(EARLY, other_step)

    def hidden_step(i):
        wd_copy(i).wait_recv()
        wf_copy(i).start()
        for h in range(2):
            if h == 1:
                wf_wait(i)
            transit(i, h)
            plain(i, h)
            keep(i, h)

        @pl.when(jnp.logical_and(even, i < 2 * EARLY))
        def _():
            for h in range(2):
                combine(i - EARLY, h)

        @pl.when(i >= EARLY + lag)
        def _():
            for h in range(2):
                combine(i - lag, h)

    loop(F_AT, hidden_step, EARLY)

    def col_wait(k):
        d_, z_ = k // 4, lax.rem(k, 4)
        block = g_col.at[d_, col_row(z_)]
        rc(block, block, col_ss.at[k], col_rs.at[k], sibling).wait_recv()

    loop(8, col_wait)
    sib_copy.wait_recv()
    n_feat = g_all.shape[2] // TILE

    def fisher_part(k, n):
        cols = pl.ds(pl.multiple_of(n * TILE, TILE), TILE)
        return dot_tn(g_all[k, :, cols], g_col[d]) + dot_tn(g_sib[k, :, cols], g_col[1 - d])

    f_copy = rc(f_out, f_in, f_ss, f_rs, partner)

    def fisher_other(n):
        f_out[pl.ds(pl.multiple_of(n * TILE, TILE), TILE), :] = fisher_part(1, n).astype(jnp.bfloat16)

    loop(n_feat, fisher_other)
    f_copy.start()

    loop(n_chunk, hidden_step, F_AT)

    def late_step(i):
        for h in range(2):
            combine(i, h)

    loop(n_chunk, late_step, n_chunk - lag)

    def fisher_own(n):
        fis_ref[pl.ds(pl.multiple_of(n * TILE, TILE), TILE), :] = fisher_part(0, n)

    loop(n_feat, fisher_own)
    fis_copy = pltpu.make_async_copy(fis_ref, fis_out, fis_s)
    fis_copy.start()

    def hidden_out(i):
        for h in range(2):
            pl_copy(i, h).wait_recv()
            cb_copy(i, h).wait_recv()
            total = own_sum[h, i] + pl_in[h, i].astype(jnp.float32) + cb_in[h, i].astype(jnp.float32)
            hid_ref[:, w_rows(i, h)] = total.astype(jnp.bfloat16)

    loop(n_chunk, hidden_out)
    f_copy.wait_recv()
    fis_copy.wait()

    for f in range(2):
        loop(16, lambda k: lab_copy(k, f).wait_send(), 1)

    def gx_done(f, s):
        near, far, _ = gx_parts(f, s)

        @pl.when(a != a_to)
        def _():
            near.wait_send()

        far.wait_send()

    for f in range(2):
        loop(n_part, lambda s: gx_done(f, s))

    def relay_done(t):
        q, f, s = unit(t)

        @pl.when(zeta != 3)
        def _():
            g_copy(first, q, f, s, 0).wait_send()

        @pl.when(zeta != 2)
        def _():
            g_copy(first, q, f, s, 1).wait_send()

    loop(4 * UNITS, relay_done)
    sib_copy.wait_send()

    def cz_done(k):
        n, is_self, mid, own, dst, sem, to = cz_parts(k)

        @pl.when(jnp.logical_not(is_self))
        def _():
            rc(mid, dst, col_ss.at[k], sem, to).wait_send()

    loop(8, cz_done)
    cy_each(lambda copy: copy.wait_send())

    def rest_done(i):
        wd_copy(i).wait_send()
        wf_copy(i).wait_send()
        for h in range(2):
            tr_copy(i, h).wait_send()
            pl_copy(i, h).wait_send()
            cb_copy(i, h).wait_send()

    loop(n_chunk, rest_done)
    f_copy.wait_send()


def fast_shards(expected, extra, row_ids, slots, unembedding, down_weight):
    tokens, feats = expected.shape
    hidden = down_weight.shape[0]
    n_chunk = hidden // 2 // TILE
    bf16, f32 = jnp.bfloat16, jnp.float32
    total_tokens = tokens * 16
    vmem, dma = pltpu.VMEM, pltpu.SemaphoreType.DMA
    chunks = (2, n_chunk, TILE, TILE)
    any_spec = pl.BlockSpec(memory_space=pl.ANY)
    vmem_spec = pl.BlockSpec(memory_space=pltpu.VMEM)
    hidden_grad, own, other = pl.pallas_call(
        kernel,
        out_shape=(
            jax.ShapeDtypeStruct((tokens, hidden), bf16),
            jax.ShapeDtypeStruct((feats, feats // 2), f32),
            jax.ShapeDtypeStruct((feats, feats // 2), bf16),
        ),
        in_specs=[vmem_spec] * 4 + [any_spec] * 2,
        out_specs=(vmem_spec, any_spec, any_spec),
        scratch_shapes=[
            vmem((DEPTH, feats), bf16),
            vmem((16 * CAP, feats), bf16),
            vmem((16 * CAP, feats), bf16),
            vmem((tokens, feats), bf16),
            vmem((2, 4 * tokens, feats), bf16),
            vmem((2, 4 * tokens, feats), bf16),
            vmem((2, 4 * tokens, feats // 2), bf16),
            vmem((3, 2, tokens, feats // 2), bf16),
            vmem((hidden, feats), bf16),
            vmem((hidden, feats), bf16),
            vmem(chunks, bf16), vmem(chunks, bf16),
            vmem(chunks, bf16), vmem(chunks, bf16),
            vmem(chunks, bf16), vmem(chunks, bf16),
            vmem(chunks, f32),
            vmem((feats, feats // 2), f32),
            vmem((feats, feats // 2), bf16),
            dma((unembedding.shape[0] // DEPTH,)), dma((2, 16)), dma((2, 16)), dma,
            dma((n_chunk,)), dma((n_chunk,)), dma((n_chunk,)), dma((n_chunk,)),
            dma((2, UNITS)), dma((8, UNITS)), dma((2, 4, UNITS)),
            dma((2, n_chunk)), dma((2, n_chunk)), dma((2, n_chunk)),
            dma((2, n_chunk)), dma((2, n_chunk)), dma((2, n_chunk)),
            dma, dma, dma((3, 2)), dma((3, 2)), dma((8,)), dma((8,)), dma, dma, dma,
        ],
        compiler_params=pltpu.CompilerParams(
            collective_id=0, has_side_effects=True, vmem_limit_bytes=60 * 1024 * 1024
        ),
    )(row_ids, slots, expected, extra, unembedding, down_weight)
    return hidden_grad, (own + other.astype(f32)) / total_tokens


def shards(expected, labels, unembedding, down_weight):
    tokens = expected.shape[0]
    voc_shard = unembedding.shape[0]
    place = lax.axis_index("dp") * lax.axis_size("col") + lax.axis_index("col")
    ids = labels.reshape(-1, tokens)
    owner = ids // voc_shard
    before = lax.broadcasted_iota(jnp.int32, (1, tokens, tokens), 1) > lax.broadcasted_iota(
        jnp.int32, (1, tokens, tokens), 2
    )
    same_label = ids[:, :, None] == ids[:, None, :]
    is_first = jnp.logical_not(jnp.any(same_label & before, axis=2))
    ahead = (owner[:, :, None] == owner[:, None, :]) & before & is_first[:, None, :]
    rank = jnp.sum(ahead.astype(jnp.int32), axis=2)
    fits = jnp.max(jnp.where(is_first, rank, 0)) < CAP
    at_slot = ((owner == place) & is_first)[:, None, :] & (
        rank[:, None, :] == lax.broadcasted_iota(jnp.int32, (1, CAP, 1), 1)
    )
    row_ids = jnp.sum(jnp.where(at_slot, (ids - place * voc_shard)[:, None, :], 0), axis=2).reshape(1, -1)

    def mine(x):
        return lax.dynamic_slice_in_dim(x, place, 1, 0)

    own_ids = mine(ids)
    holds = (own_ids.reshape(tokens, 1) == own_ids) & mine(is_first).reshape(tokens, 1)
    slots = jnp.sum(jnp.where(holds, mine(owner * CAP + rank).reshape(tokens, 1), 0), axis=0, keepdims=True)
    extra = lax.cond(
        fits,
        lambda: jnp.zeros_like(expected),
        lambda: dense_rows(ids, unembedding, place),
    )
    slots = jnp.where(fits, slots, -1)
    return fast_shards(expected, extra, row_ids, slots, unembedding, down_weight)


def solution(mesh):
    in_specs = (P(("dp", "col"), "row"), P(), P(("dp", "col"), "row"), P("col", "row"))
    out_specs = (P(("dp", "row"), "col"), P("row", ("dp", "col")))
    return jax.shard_map(shards, mesh=mesh, in_specs=in_specs, out_specs=out_specs, check_vma=False)
```

time: 892 us -> 160 us (0.18)
  waiting for transfers between devices: 695 us -> 0 us
  Pallas kernels: 0 us -> 147 us
  blocking collectives: 99.9 us -> 0 us
  local copies, waits for them, and re-layouts: 32.3 us -> 2.69 us
  matrix products: 28.9 us -> 0 us
  between operations: 13.8 us -> 1.36 us
  other arithmetic: 20.6 us -> 8.29 us
    psum x1 -> x0, waiting for transfers between devices: 365 us -> none  [shards(): lax.psum(jnp.where(inside_shard[:, None], picked.astype(jnp.float32), 0.0...]
    reduce_scatter x1 -> x0, waiting for transfers between devices: 226 us -> none  [shards(): lax.psum_scatter(lax.dot_general(replica_panel, down_weight, contract_las...]
    pallas_call x0 -> x1, Pallas kernels: none -> 147 us  [fast_shards(): pl.pallas_call(kernel, out_shape=(jax.ShapeDtypeStruct((tokens, hidden),...]
    all_gather x2 -> x0, waiting for transfers between devices: 103 us -> none  [the longest x1 73.3 us: shards(): gathered = lax.all_gather(expected, ('dp', 'col'), axis=0, tiled=True)]
    all_to_all x1 -> x0, blocking collectives: 99.9 us -> none  [shards(): lax.all_to_all(wide_tile, ('dp', 'col'), split_axis=1, concat_axis=0, til...]
    dot_general x2 -> x0, matrix products: 28.9 us -> none  [the longest x1 23.1 us: shards(): lax.dot_general(replica_panel, down_weight, contract_last, preferred_elem...]
    gather x1 -> x0, local copies, waits for them, and re-layouts: 25.3 us -> none  [shards(): jnp.take(unembedding, jnp.clip(local_ids, 0, voc_shard - 1), axis=0)]
    convert_element_type x3 -> x0, other arithmetic: 19.2 us -> none  [the longest x1 7.88 us: shards(): grad_all = (gathered.astype(jnp.float32) - label_sum).astype(jnp.bfloat16)]
  transfers between devices with their start and end apart: 4 -> 0, of which waited for: 4 -> 0; matrix products, arithmetic and copies ran while one was open for 4% -> 0% of each run, Pallas kernels for 0% -> 0%
where the time goes in v1:
time: 160 us; the launch traced here: 159 us
  Pallas kernels  147 us (92%)
  other arithmetic  8.29 us (5%)
  local copies, waits for them, and re-layouts  2.69 us (2%)
    pallas_call x1, Pallas kernels, fast_shards(): pl.pallas_call(kernel, out_shape=(jax.ShapeDtypeStruct((tokens, hidden),...  147 us
    div x1, other arithmetic, fast_shards(): return (hidden_grad, (own + other.astype(f32)) / total_tokens)  3.64 us

profile of v1, /device:TPU:38, one launch (start us, length us, event | category | flops | bytes accessed | tf_op | source)
XLA Modules:
  0.0 159.5 jit_solution(17134833172899297224)
XLA Ops:
  0.6 0.7 reshape.189
  1.4 1.3 and_reduce_fusion.2
  2.7 1.5 convert_reduce_fusion
  4.3 0.6 select_reduce_fusion.2
  5.6 0.4 select_reduce_fusion
  5.9 0.7 reshape.190.row_ref
  6.6 0.2 select_reduce_fusion.1
  6.8 0.6 broadcast_select_fusion.1
  7.4 0.1 conditional.1
  7.4 0.1 broadcast.249
  7.4 147.2 %shard_map.59 = (bf16[256,3584]{1,0:T(8,128)(2,1)}, f32[1024,512]{1,0:T(8,128)}, bf16[1024,512]{1,0:T(8,128)(2,1)}) custom-call(s32[1,512]{1,0:T(1,128)} %reshape.190.row_ref, s32[1,256]{1,0:T(1,128)} %bitcast.9, bf16[256,1024]{1,0:T(8,128)(2,1)} %exp_ref.1, bf16[256,1024]{1,0:T(8,128)(2,1)S(1)} %get-tuple-element.243.extra_ref, bf16[4096,1024]{1,0:T(8,128)(2,1)} %u_ref.1, ...), custom_call_target="tpu_custom_call" | custom-call | tf_op jit(solution)/shard_map/pallas_call | solution.py:544
  154.6 0.0 copy-start
  154.6 3.6 %add_multiply_fusion = f32[1024,512]{1,0:T(8,128)} fusion(f32[1024,512]{1,0:T(8,128)} %get-tuple-element.153, bf16[1024,512]{1,0:T(8,128)(2,1)} %get-tuple-element.154), kind=kLoop, calls=%fused_computation.14 | loop fusion | flops 1572864 | bytes 5242880 | tf_op jit(solution)/shard_map/div | solution.py:581
  158.3 0.0 copy-done
  158.3 1.2 copy.15
  (5 shorter events, 0.1 us)
Async XLA Ops:
  154.6 3.7 %copy-start = (bf16[256,3584]{1,0:T(8,128)(2,1)S(1)}, bf16[256,3584]{1,0:T(8,128)(2,1)}, u32[]{:S(2)}) copy-start(bf16[256,3584]{1,0:T(8,128)(2,1)} %get-tuple-element.241) | copy-start | bytes 5505028

commit v2 on v1

--- a/solution.py
+++ b/solution.py
@@ -361,9 +361,6 @@
             loop((3 + i) * UNITS, relay, (2 + i) * UNITS)
 
     loop(EARLY, early_step)
-    loop(4 * UNITS, second_wait, 2 * UNITS)
-    sib_copy = rc(g_all, g_sib, sib_ss, sib_rs, sibling)
-    sib_copy.start()
 
     def cz_parts(k):
         n, d_ = k // 2, lax.rem(k, 2)
@@ -387,8 +384,18 @@
             def _():
                 rc(src, dst, col_ss.at[k], sem, to).start()
 
-    cy_each(lambda copy: copy.wait_recv())
-    loop(8, cz_start)
+    loop(2, cz_start)
+    loop(4 * UNITS, second_wait, 2 * UNITS)
+    sib_copy = rc(g_all, g_sib, sib_ss, sib_rs, sibling)
+    sib_copy.start()
+
+    def cz_pass(i):
+        n = jnp.where(i == 2, 2, 1 + 2 * i)
+        for d_ in range(2):
+            cy_copy(n, d_).wait_recv()
+            cz_start(2 * n + d_)
+
+    loop(3, cz_pass)
 
     lag = 1
 

time: 160 us -> 160 us (level)
  no operation moved by 1% of the time
where the time goes in v2:
time: 160 us; the launch traced here: 159 us
  Pallas kernels  147 us (92%)
  other arithmetic  8.29 us (5%)
  local copies, waits for them, and re-layouts  2.69 us (2%)
    pallas_call x1, Pallas kernels, fast_shards(): pl.pallas_call(kernel, out_shape=(jax.ShapeDtypeStruct((tokens, hidden),...  147 us
    div x1, other arithmetic, fast_shards(): return (hidden_grad, (own + other.astype(f32)) / total_tokens)  3.64 us

profile of v2, /device:TPU:38, one launch (start us, length us, event | category | flops | bytes accessed | tf_op | source)
XLA Modules:
  0.0 159.5 jit_solution(13928216427367708095)
XLA Ops:
  0.6 0.7 reshape.189
  1.4 1.3 and_reduce_fusion.2
  2.7 1.5 convert_reduce_fusion
  4.3 0.6 select_reduce_fusion.2
  5.6 0.4 select_reduce_fusion
  5.9 0.7 reshape.190.row_ref
  6.6 0.2 select_reduce_fusion.1
  6.8 0.6 broadcast_select_fusion.1
  7.4 0.1 conditional.1
  7.4 0.1 broadcast.249
  7.4 147.2 %shard_map.59 = (bf16[256,3584]{1,0:T(8,128)(2,1)}, f32[1024,512]{1,0:T(8,128)}, bf16[1024,512]{1,0:T(8,128)(2,1)}) custom-call(s32[1,512]{1,0:T(1,128)} %reshape.190.row_ref, s32[1,256]{1,0:T(1,128)} %bitcast.9, bf16[256,1024]{1,0:T(8,128)(2,1)} %exp_ref.1, bf16[256,1024]{1,0:T(8,128)(2,1)S(1)} %get-tuple-element.243.extra_ref, bf16[4096,1024]{1,0:T(8,128)(2,1)} %u_ref.1, ...), custom_call_target="tpu_custom_call" | custom-call | tf_op jit(solution)/shard_map/pallas_call | solution.py:551
  154.6 0.0 copy-start
  154.6 3.6 %add_multiply_fusion = f32[1024,512]{1,0:T(8,128)} fusion(f32[1024,512]{1,0:T(8,128)} %get-tuple-element.153, bf16[1024,512]{1,0:T(8,128)(2,1)} %get-tuple-element.154), kind=kLoop, calls=%fused_computation.14 | loop fusion | flops 1572864 | bytes 5242880 | tf_op jit(solution)/shard_map/div | solution.py:588
  158.3 0.0 copy-done
  158.3 1.2 copy.15
  (5 shorter events, 0.1 us)
Async XLA Ops:
  154.6 3.7 %copy-start = (bf16[256,3584]{1,0:T(8,128)(2,1)S(1)}, bf16[256,3584]{1,0:T(8,128)(2,1)}, u32[]{:S(2)}) copy-start(bf16[256,3584]{1,0:T(8,128)(2,1)} %get-tuple-element.241) | copy-start | bytes 5505028
